TPU v7x, 32 devices: a whole 2x2x4 slice. The times are simulated.
32 devices in a mesh: wall: 2 (over core), sx: 4 (over y, x), sy: 4 (over z).
Axes of the slice: x: 2, y: 2, z: 4, core: 2. Of those that a mesh axis runs over, the one named last changes fastest.
Arguments:
- forcing: float32 [4, 8, 8, 384], P('sx', 'sy', 'wall'), may hold values from -17 to 17
- pivot_inverse: float32 [4, 8, 8, 384, 384], P('sx', 'sy', 'wall'), may hold values from -1 to 5
- lower_face: float32 [4, 8, 8, 96, 96], P('sx', 'sy', 'wall'), may hold values from -1 to 2
- upper_face: float32 [4, 8, 8, 96, 96], P('sx', 'sy', 'wall'), may hold values from -1 to 2
- side_coupling: float32 [4, 8, 8, 4, 96, 96], P('sx', 'sy', 'wall'), may hold values from -0.3125 to 0.3125
- orientation: int32 [4, 8, 8, 4], P('sx', 'sy', 'wall'), may hold values from 0 to 3
Outputs:
- solution: float32 [4, 8, 8, 384], P('sx', 'sy', 'wall')
- relative_residual: float32 [], replicated
- forcing_rms: float32 [], replicated
All inputs are finite; a program needn't handle non-finite values.
Results may differ from a plain program's by a relative error of at most 0.0003.
Values sent between devices are 32-bit elements; how exact they have to be, the bound alone decides.
A program may use at most 64 MiB of HBM per device.

v0:
```python
import jax
import jax.numpy as jnp
from jax import lax
from jax.sharding import PartitionSpec as P

PTS = 4
VARS = 6
BLOCK = 384
FACE = 96
ITERS = 3


precise = lax.Precision.HIGHEST


def entering(part, axis, combine, identity, reverse):
    count = lax.axis_size(axis)
    place = lax.axis_index(axis)
    ahead = count - 1 - place if reverse else place
    gathered = jax.tree.map(lambda a: lax.all_gather(a, axis), part)
    state = jax.tree.map(lambda a, e: jnp.zeros_like(a) + jnp.asarray(e, a.dtype), part, identity)

    def one(step, state):
        source = count - 1 - step if reverse else step
        return combine(
            state, jax.tree.map(lambda a: lax.dynamic_index_in_dim(a, source, 0, False), gathered)
        )

    return lax.fori_loop(0, ahead, one, state)


def extended(block, sides, width):
    for axis, dim in sides:
        count = lax.axis_size(axis)
        forward = [(i, i + 1) for i in range(count - 1)]
        backward = [(target, source) for source, target in forward]
        low = lax.ppermute(
            lax.slice_in_dim(block, block.shape[dim] - width, None, axis=dim), axis, forward
        )
        high = lax.ppermute(lax.slice_in_dim(block, 0, width, axis=dim), axis, backward)
        block = jnp.concatenate([low, block, high], axis=dim)
    return block


def face_traces(vector_in):
    leading = vector_in.shape[:-1]
    node_grid = vector_in.reshape(leading + (PTS, PTS, PTS, VARS))
    facets = [
        node_grid[..., :, :, 0, :],
        node_grid[..., :, :, PTS - 1, :],
        node_grid[..., :, 0, :, :],
        node_grid[..., :, PTS - 1, :, :],
    ]
    flattened = [one_facet.reshape(leading + (FACE,)) for one_facet in facets]
    return jnp.stack(flattened, -2).reshape(leading + (4 * FACE,))


def lateral_term(vector_in, padded, side_coupling, orientation):
    single_row_block, rows_two = (vector_in.shape[0], vector_in.shape[1])
    beside_all = padded.reshape(padded.shape[:3] + (4, FACE))
    across = jnp.stack(
        [
            beside_all[0:single_row_block, 1 : rows_two + 1, :, 1],
            beside_all[2 : single_row_block + 2, 1 : rows_two + 1, :, 0],
            beside_all[1 : single_row_block + 1, 0:rows_two, :, 3],
            beside_all[1 : single_row_block + 1, 2 : rows_two + 2, :, 2],
        ],
        3,
    )
    shaped = across.reshape(across.shape[:4] + (PTS, PTS, VARS))
    turned = jnp.zeros(shaped.shape, jnp.float32)
    for quarter in range(4):
        picked = (orientation == quarter).astype(jnp.float32)[..., None, None, None]
        turned = turned + picked * jnp.rot90(shaped, quarter, axes=(4, 5))
    coupled = jnp.einsum(
        "xyefab,xyefb->xyefa", side_coupling, turned.reshape(across.shape), precision=precise
    )
    pieces = coupled.reshape(across.shape[:4] + (PTS, PTS, VARS))
    result = jnp.zeros(vector_in.shape[:3] + (PTS, PTS, PTS, VARS), jnp.float32)
    result = result.at[:, :, :, :, :, 0, :].add(pieces[:, :, :, 0])
    result = result.at[:, :, :, :, :, PTS - 1, :].add(pieces[:, :, :, 1])
    result = result.at[:, :, :, :, 0, :, :].add(pieces[:, :, :, 2])
    result = result.at[:, :, :, :, PTS - 1, :, :].add(pieces[:, :, :, 3])
    return result.reshape(vector_in.shape)


def apply_map(matrix, vector):
    return jnp.einsum("xyab,xyb->xya", matrix, vector, precision=precise)


def compose(earlier, later):
    return (
        jnp.einsum("xyab,xybc->xyac", later[0], earlier[0], precision=precise),
        apply_map(later[0], earlier[1]) + later[1],
    )


def pass_lower(outgoing, lower_total, identity):
    mapped = entering(
        (lower_total, outgoing), "wall", compose, (identity, jnp.zeros_like(outgoing)), False
    )
    return mapped[1]


def pass_upper(outgoing, upper_total, identity):
    mapped = entering(
        (upper_total, outgoing), "wall", compose, (identity, jnp.zeros_like(outgoing)), True
    )
    return mapped[1]


def solve_small(matrix, vector):
    extent = matrix.shape[0]
    index_ids = jnp.arange(extent)
    for k in range(extent):
        factor_col = jnp.where(index_ids > k, matrix[:, k] / matrix[k, k], 0.0)
        matrix = matrix - factor_col[:, None] * matrix[k][None, :]
        vector = vector - factor_col * vector[k]
    solved = jnp.zeros((extent,), jnp.float32)
    for k in reversed(range(extent)):
        solved = solved.at[k].set((vector[k] - jnp.sum(matrix[k] * solved)) / matrix[k, k])
    return solved


def least_squares(hessenberg, initial_norm):
    target = jnp.zeros((hessenberg.shape[0],), jnp.float32).at[0].set(initial_norm)
    normal = jnp.dot(hessenberg.T, hessenberg, precision=precise)
    weights = solve_small(normal, jnp.dot(hessenberg.T, target, precision=precise))
    misfit = target - jnp.dot(hessenberg, weights, precision=precise)
    return (weights, jnp.sqrt(jnp.sum(misfit * misfit)) / initial_norm)


def shards(forcing, pivot_inverse, lower_face, upper_face, side_coupling, orientation):
    elements = forcing.shape[2]
    lower_maps = -jnp.einsum(
        "xyeab,xyebc->xyeac",
        pivot_inverse[..., BLOCK - FACE :, :FACE],
        lower_face,
        precision=precise,
    )
    upper_maps = -jnp.einsum(
        "xyeab,xyebc->xyeac",
        pivot_inverse[..., :FACE, BLOCK - FACE :],
        upper_face,
        precision=precise,
    )
    identity = jnp.broadcast_to(jnp.eye(FACE, dtype=jnp.float32), forcing.shape[:2] + (FACE, FACE))
    lower_total = identity
    for i in range(elements):
        lower_total = jnp.einsum(
            "xyab,xybc->xyac", lower_maps[:, :, i], lower_total, precision=precise
        )
    upper_total = identity
    for i in reversed(range(elements)):
        upper_total = jnp.einsum(
            "xyab,xybc->xyac", upper_maps[:, :, i], upper_total, precision=precise
        )
    squares = lax.psum(jnp.sum(forcing * forcing), ("wall", "sx", "sy"))
    entry_count = forcing.size * lax.axis_size("wall") * lax.axis_size("sx") * lax.axis_size("sy")
    forcing_rms = jnp.sqrt(squares / entry_count)
    initial_norm = jnp.sqrt(squares)
    krylov = [forcing / initial_norm]
    directions = []
    columns = []
    for j in range(ITERS):
        resid = krylov[j]
        ahead_part = jnp.einsum(
            "xyeab,xyeb->xyea", pivot_inverse[..., BLOCK - FACE :, :], resid, precision=precise
        )
        carried = jnp.zeros(resid.shape[:2] + (FACE,), jnp.float32)
        for precondition_i in range(elements):
            carried = ahead_part[:, :, precondition_i] + apply_map(
                lower_maps[:, :, precondition_i], carried
            )
        carried = pass_lower(carried, lower_total, identity)
        rows_out = []
        for precondition_i in range(elements):
            lowered = apply_map(lower_face[:, :, precondition_i], carried)
            rows_out.append(
                jnp.concatenate(
                    [
                        resid[:, :, precondition_i, :FACE] - lowered,
                        resid[:, :, precondition_i, FACE:],
                    ],
                    -1,
                )
            )
            carried = ahead_part[:, :, precondition_i] + apply_map(
                lower_maps[:, :, precondition_i], carried
            )
        reduced = jnp.stack(rows_out, 2)
        trailing_rows = jnp.einsum(
            "xyeab,xyeb->xyea", pivot_inverse[..., :FACE, :], reduced, precision=precise
        )
        carried = jnp.zeros(resid.shape[:2] + (FACE,), jnp.float32)
        for precondition_i in reversed(range(elements)):
            carried = trailing_rows[:, :, precondition_i] + apply_map(
                upper_maps[:, :, precondition_i], carried
            )
        carried = pass_upper(carried, upper_total, identity)
        rows_back = [None] * elements
        for precondition_i in reversed(range(elements)):
            raised = apply_map(upper_face[:, :, precondition_i], carried)
            rows_back[precondition_i] = jnp.concatenate(
                [
                    reduced[:, :, precondition_i, : BLOCK - FACE],
                    reduced[:, :, precondition_i, BLOCK - FACE :] - raised,
                ],
                -1,
            )
            carried = trailing_rows[:, :, precondition_i] + apply_map(
                upper_maps[:, :, precondition_i], carried
            )
        direction = jnp.einsum(
            "xyeab,xyeb->xyea", pivot_inverse, jnp.stack(rows_back, 2), precision=precise
        )
        directions.append(direction)
        traces = face_traces(direction)
        padded = extended(traces, (("sx", 0), ("sy", 1)), 1)
        vector_w = krylov[j] + lateral_term(direction, padded, side_coupling, orientation)
        listed = []
        for i in range(j + 1):
            projected = lax.psum(jnp.sum(vector_w * krylov[i]), ("wall", "sx", "sy"))
            vector_w = vector_w - projected * krylov[i]
            listed.append(projected)
        coeffs = jnp.stack(listed)
        length = jnp.sqrt(lax.psum(jnp.sum(vector_w * vector_w), ("wall", "sx", "sy")))
        krylov.append(vector_w / length)
        columns.append(
            jnp.concatenate([coeffs, length[None], jnp.zeros((ITERS - 1 - j,), jnp.float32)])
        )
    hessenberg = jnp.stack(columns, 1)
    weights, relative = least_squares(hessenberg, initial_norm)
    solution = weights[0] * directions[0]
    for j in range(1, ITERS):
        solution = solution + weights[j] * directions[j]
    return (solution, relative, forcing_rms)


def solution(mesh):
    return jax.shard_map(
        shards,
        mesh=mesh,
        in_specs=(
            P("sx", "sy", "wall", None),
            P("sx", "sy", "wall", None, None),
            P("sx", "sy", "wall", None, None),
            P("sx", "sy", "wall", None, None),
            P("sx", "sy", "wall", None, None, None),
            P("sx", "sy", "wall", None),
        ),
        out_specs=(P("sx", "sy", "wall", None), P(), P()),
        check_vma=False,
    )
```

profile of v0, /device:TPU:0, one launch (start us, length us, event | category | flops | bytes accessed | tf_op | source)
XLA Modules:
  0.0 700.6 jit_solution(9128759101359611290)
XLA Ops:
  2.2 42.2 %psum.70 = f32[]{:T(128)} all-reduce(f32[]{:T(128)} %multiply_reduce_fusion.9), channel_id=1, replica_groups=mesh['wall'=2,'sx'=4,'sy'=4] {'wall','sx','sy'}, use_global_device_ids=true, to_apply=%region_1.0 | all-reduce | flops 1 | bytes 8 | tf_op jit(solution)/shard_map/psum | solution.py:158
  79.1 6.6 fusion.34
  89.4 4.2 collective-permute-start
  94.9 4.2 collective-permute-done.1
  104.6 3.6 collective-permute-done.3
  133.3 39.8 %psum.71 = f32[]{:T(128)} all-reduce(f32[]{:T(128)} %get-tuple-element.783), channel_id=1, replica_groups=mesh['wall'=2,'sx'=4,'sy'=4] {'wall','sx','sy'}, use_global_device_ids=true, to_apply=%region_7.8 | all-reduce | flops 1 | bytes 8 | tf_op jit(solution)/shard_map/psum | solution.py:223
  175.1 41.1 %psum.72 = f32[]{:T(128)} all-reduce(f32[]{:T(128)} %multiply_reduce_fusion.7), channel_id=1, replica_groups=mesh['wall'=2,'sx'=4,'sy'=4] {'wall','sx','sy'}, use_global_device_ids=true, to_apply=%region_9.10 | all-reduce | flops 1 | bytes 8 | tf_op jit(solution)/shard_map/psum | solution.py:227
  242.5 4.0 all-gather.11
  260.4 6.6 fusion.32
  271.3 4.2 collective-permute-start.4
  276.9 4.2 collective-permute-done.5
  285.9 4.1 collective-permute-done.7
  314.1 39.2 %psum.73 = f32[]{:T(128)} all-reduce(f32[]{:T(128)} %get-tuple-element.781), channel_id=1, replica_groups=mesh['wall'=2,'sx'=4,'sy'=4] {'wall','sx','sy'}, use_global_device_ids=true, to_apply=%region_15.16 | all-reduce | flops 1 | bytes 8 | tf_op jit(solution)/shard_map/psum | solution.py:223
  355.3 41.7 %psum.74 = f32[]{:T(128)} all-reduce(f32[]{:T(128)} %multiply_reduce_fusion.5), channel_id=1, replica_groups=mesh['wall'=2,'sx'=4,'sy'=4] {'wall','sx','sy'}, use_global_device_ids=true, to_apply=%region_17.18 | all-reduce | flops 1 | bytes 8 | tf_op jit(solution)/shard_map/psum | solution.py:223
  400.1 39.2 %psum.75 = f32[]{:T(128)} all-reduce(f32[]{:T(128)} %get-tuple-element.779), channel_id=1, replica_groups=mesh['wall'=2,'sx'=4,'sy'=4] {'wall','sx','sy'}, use_global_device_ids=true, to_apply=%region_19.20 | all-reduce | flops 1 | bytes 8 | tf_op jit(solution)/shard_map/psum | solution.py:227
  464.3 3.8 all-gather.13
  471.2 6.6 fusion.30
  479.2 4.2 collective-permute-start.8
  484.8 4.2 collective-permute-done.9
  494.2 3.7 collective-permute-done.11
  505.2 39.2 %psum.76 = f32[]{:T(128)} all-reduce(f32[]{:T(128)} %get-tuple-element.777), channel_id=1, replica_groups=mesh['wall'=2,'sx'=4,'sy'=4] {'wall','sx','sy'}, use_global_device_ids=true, to_apply=%region_25.26 | all-reduce | flops 1 | bytes 8 | tf_op jit(solution)/shard_map/psum | solution.py:223
  545.7 41.8 %psum.77 = f32[]{:T(128)} all-reduce(f32[]{:T(128)} %multiply_reduce_fusion.2), channel_id=1, replica_groups=mesh['wall'=2,'sx'=4,'sy'=4] {'wall','sx','sy'}, use_global_device_ids=true, to_apply=%region_27.28 | all-reduce | flops 1 | bytes 8 | tf_op jit(solution)/shard_map/psum | solution.py:223
  590.2 39.2 %psum.78 = f32[]{:T(128)} all-reduce(f32[]{:T(128)} %multiply_reduce_fusion.1), channel_id=1, replica_groups=mesh['wall'=2,'sx'=4,'sy'=4] {'wall','sx','sy'}, use_global_device_ids=true, to_apply=%region_29.30 | all-reduce | flops 1 | bytes 8 | tf_op jit(solution)/shard_map/psum | solution.py:223
  633.3 41.6 %psum.79 = f32[]{:T(128)} all-reduce(f32[]{:T(128)} %multiply_reduce_fusion), channel_id=1, replica_groups=mesh['wall'=2,'sx'=4,'sy'=4] {'wall','sx','sy'}, use_global_device_ids=true, to_apply=%region_31.32 | all-reduce | flops 1 | bytes 8 | tf_op jit(solution)/shard_map/psum | solution.py:227
  (482 shorter events, 220.5 us)
Async XLA Ops:
  0.6 113.4 %copy-start = (f32[1,2,4,4,96,96]{5,4,3,2,1,0:T(8,128)S(1)}, f32[1,2,4,4,96,96]{5,4,3,2,1,0:T(8,128)}, u32[]{:S(2)}) copy-start(f32[1,2,4,4,96,96]{5,4,3,2,1,0:T(8,128)} %param.54) | copy-start | bytes 3538948
  0.6 57.4 %copy-start.1 = (f32[1,2,4,96,96]{4,3,2,1,0:T(8,128)S(1)}, f32[1,2,4,96,96]{4,3,2,1,0:T(8,128)}, u32[]{:S(2)}) copy-start(f32[1,2,4,96,96]{4,3,2,1,0:T(8,128)} %param.52) | copy-start | bytes 884740
  0.7 58.2 %copy-start.2 = (f32[1,2,4,96,96]{4,3,2,1,0:T(8,128)S(1)}, f32[1,2,4,96,96]{4,3,2,1,0:T(8,128)}, u32[]{:S(2)}) copy-start(f32[1,2,4,96,96]{4,3,2,1,0:T(8,128)} %param.53) | copy-start | bytes 884740
  88.0 43.4 %copy-start.5 = (f32[1,2,4,384]{3,2,1,0:T(4,128)S(1)}, f32[1,2,4,384]{3,2,1,0:T(4,128)}, u32[]{:S(2)}) copy-start(f32[1,2,4,384]{3,2,1,0:T(4,128)} %param.50) | copy-start | bytes 36868
  89.4 5.6 collective-permute-start
  93.6 5.6 collective-permute-start.1
  99.2 5.4 collective-permute-start.2
  102.6 5.7 collective-permute-start.3
  114.0 138.0 %copy-start.3 = (f32[1,2,4,96,96]{4,3,2,1,0:T(8,128)S(1)}, f32[1,2,4,96,96]{4,3,2,1,0:T(8,128)}, u32[]{:S(2)}) copy-start(f32[1,2,4,96,96]{4,3,2,1,0:T(8,128)} %param.53) | copy-start | bytes 884740
  271.3 5.6 collective-permute-start.4
  275.5 5.6 collective-permute-start.5
  281.1 4.8 collective-permute-start.6
  284.4 5.7 collective-permute-start.7
  294.7 174.7 %copy-start.4 = (f32[1,2,4,96,96]{4,3,2,1,0:T(8,128)S(1)}, f32[1,2,4,96,96]{4,3,2,1,0:T(8,128)}, u32[]{:S(2)}) copy-start(f32[1,2,4,96,96]{4,3,2,1,0:T(8,128)} %param.53) | copy-start | bytes 884740
  468.6 30.5 %copy-start.14 = (f32[2,4,4]{2,1,0:T(4,128)S(1)}, f32[2,4,4]{2,1,0:T(4,128)}, u32[]{:S(2)}) copy-start(f32[2,4,4]{2,1,0:T(4,128)} %copy-done.13) | copy-start | bytes 388
  468.6 30.5 %copy-start.16 = (f32[2,4,4]{2,1,0:T(4,128)S(1)}, f32[2,4,4]{2,1,0:T(4,128)}, u32[]{:S(2)}) copy-start(f32[2,4,4]{2,1,0:T(4,128)} %copy-done.15) | copy-start | bytes 388
  468.6 30.5 %copy-start.18 = (f32[2,4,4]{2,1,0:T(4,128)S(1)}, f32[2,4,4]{2,1,0:T(4,128)}, u32[]{:S(2)}) copy-start(f32[2,4,4]{2,1,0:T(4,128)} %copy-done.17) | copy-start | bytes 388
  478.2 66.2 %copy-start.7 = (f32[1,1,8,384]{3,2,1,0:T(8,128)S(1)}, f32[1,1,8,384]{3,2,1,0:T(8,128)}, u32[]{:S(2)}) copy-start(f32[1,1,8,384]{3,2,1,0:T(8,128)} %copy-done.6) | copy-start | bytes 36868
  478.6 217.4 %copy-start.10 = (f32[2,4,1,384]{3,2,1,0:T(1,128)S(1)}, f32[2,4,1,384]{3,2,1,0:T(1,128)}, u32[]{:S(2)}) copy-start(f32[2,4,1,384]{3,2,1,0:T(1,128)} %copy-done.9) | copy-start | bytes 36868
  478.6 217.4 %copy-start.12 = (f32[2,4,1,384]{3,2,1,0:T(1,128)S(1)}, f32[2,4,1,384]{3,2,1,0:T(1,128)}, u32[]{:S(2)}) copy-start(f32[2,4,1,384]{3,2,1,0:T(1,128)} %copy-done.11) | copy-start | bytes 36868
  479.2 5.6 collective-permute-start.8
  483.4 5.6 collective-permute-start.9
  489.0 5.2 collective-permute-start.10
  492.2 5.7 collective-permute-start.11
  (19 other events, 91.4 us)
where the time goes:
time: 711 us; the launch traced here: 701 us
  blocking collectives  425 us (60%)
  matrix products  72.3 us (10%)
  other arithmetic  71.4 us (10%)
  local copies, waits for them, and re-layouts  62.6 us (9%)
  starting transfers between devices  30.4 us (4%)
  waiting for transfers between devices  24.3 us (3%)
  between operations  14.3 us (2%)
    psum x6, blocking collectives, shards(): projected = lax.psum(jnp.sum(vector_w * krylov[i]), ('wall', 'sx', 'sy'))  241 us
    psum x3, blocking collectives, shards(): lax.psum(jnp.sum(vector_w * vector_w), ('wall', 'sx', 'sy'))  122 us
    psum x1, blocking collectives, shards(): squares = lax.psum(jnp.sum(forcing * forcing), ('wall', 'sx', 'sy'))  42.2 us
    ppermute x6, waiting for transfers between devices, extended(): lax.ppermute(lax.slice_in_dim(block, 0, width, axis=dim), axis, backward)  24 us
    ppermute x6, starting transfers between devices, extended(): lax.ppermute(lax.slice_in_dim(block, block.shape[dim] - width, None, axis...  22.4 us
    dot_general x65, matrix products, apply_map(): return jnp.einsum('xyab,xyb->xya', matrix, vector, precision=precise)  21.5 us
    dot_general x3, matrix products, shards(): jnp.einsum('xyeab,xyeb->xyea', pivot_inverse, jnp.stack(rows_back, 2), pr...  19.8 us
    all_gather x8, blocking collectives, entering(): gathered = jax.tree.map(lambda a: lax.all_gather(a, axis), part)  19.4 us
  transfers between devices with their start and end apart: 12, of which 9 were waited for; matrix products, arithmetic and copies ran while one was open for 0% of the time, Pallas kernels for 0%

commit v1 on v0

v1 whole, which is shorter than its diff:
```python
import functools

import jax
import jax.numpy as jnp
import numpy as np
from jax import lax
from jax.experimental import pallas as pl
from jax.experimental.pallas import tpu as pltpu
from jax.sharding import PartitionSpec as P

PTS = 4
VARS = 6
BLOCK = 384
FACE = 96
ITERS = 3
LANES = 128
TAIL = BLOCK - FACE
MESH = pl.DeviceIdType.MESH
PAIRS = [(a, b) for a in range(ITERS + 1) for b in range(a, ITERS + 1)]


def face_nodes():
    ids = np.arange(BLOCK).reshape(PTS, PTS, PTS, VARS)
    return [ids[:, :, 0], ids[:, :, PTS - 1], ids[:, 0], ids[:, PTS - 1]]


def gather_matrices():
    faces = face_nodes()
    out = np.zeros((4, BLOCK, 4 * LANES), np.float32)
    for f, touching in enumerate((1, 0, 3, 2)):
        for turn in range(4):
            source = np.rot90(faces[touching], turn, axes=(0, 1)).reshape(-1)
            out[f, source, turn * LANES + np.arange(FACE)] = 1.0
    return out


def scatter_matrix():
    out = np.zeros((4 * FACE, BLOCK), np.float32)
    for f, nodes in enumerate(face_nodes()):
        out[f * FACE + np.arange(FACE), nodes.reshape(-1)] = 1.0
    return out


def split_rows(x):
    high = x.astype(jnp.bfloat16).astype(jnp.float32)
    rest = x - high
    middle = rest.astype(jnp.bfloat16).astype(jnp.float32)
    low = rest - middle
    pad = jnp.zeros_like(x)
    return jnp.concatenate([high, middle, low, pad], 0).astype(jnp.bfloat16)


def select_dot(x, chosen):
    rows = x.shape[0]
    y = jnp.dot(split_rows(x), chosen, preferred_element_type=jnp.float32)
    return y[:rows] + y[rows : 2 * rows] + y[2 * rows : 3 * rows]


def kernel(
    dims,
    total_entries,
    f_hbm,
    piv_hbm,
    low_hbm,
    up_hbm,
    side_hbm,
    ori_hbm,
    gat_hbm,
    sca_hbm,
    sol_ref,
    rel_ref,
    rms_ref,
    f_v,
    piv,
    low,
    up,
    side,
    ori,
    gat,
    sca,
    turned,
    ubuf,
    dbuf,
    yrow,
    fwd_out,
    fwd_in,
    bwd_out,
    bwd_in,
    hx_low,
    hx_high,
    hy_low,
    hy_high,
    gram_a,
    gram_b,
    load_sem,
    piv_sem,
    wall_sem,
    halo_sem,
    a_send,
    a_recv,
    b_send,
    b_recv,
):
    W, SX, SY = dims
    X, Y, E = f_v.shape[:3]
    L = X * Y
    N = L * E
    lines = [(x, y) for x in range(X) for y in range(Y)]
    wall, sx, sy = lax.axis_index("wall"), lax.axis_index("sx"), lax.axis_index("sy")
    rank = wall * SX + sx
    n_a = W * SX

    loads = [
        pltpu.make_async_copy(src, dst, load_sem.at[i])
        for i, (src, dst) in enumerate(
            [
                (f_hbm, f_v),
                (low_hbm, low),
                (up_hbm, up),
                (gat_hbm, gat),
                (side_hbm, side),
                (ori_hbm, ori),
                (sca_hbm, sca),
            ]
        )
    ]
    piv_loads = [
        pltpu.make_async_copy(piv_hbm.at[x, y, k], piv.at[x, y, k], piv_sem.at[(x * Y + y) * E + k])
        for x, y in lines
        for k in range(E)
    ]
    loads[0].start()
    for c in piv_loads:
        c.start()
    for c in loads[1:]:
        c.start()

    for ref in (fwd_in, bwd_in, hx_low, hx_high, hy_low, hy_high, fwd_out, bwd_out):
        ref[...] = jnp.zeros(ref.shape, jnp.float32)

    barrier = pltpu.get_barrier_semaphore()

    def group_a(t):
        target = lax.rem(rank + t, n_a)
        return {"wall": target // SX, "sx": lax.rem(target, SX)}

    def group_b(t):
        return {"sy": lax.rem(sy + t, SY)}

    for t in range(1, n_a):
        pl.semaphore_signal(barrier, inc=1, device_id=group_a(t), device_id_type=MESH)
    for t in range(1, SY):
        pl.semaphore_signal(barrier, inc=1, device_id=group_b(t), device_id_type=MESH)

    loads[0].wait()
    ubuf[0] = jnp.concatenate([f_v[x, y] for x, y in lines], 0)
    lane = lax.broadcasted_iota(jnp.int32, (1, LANES), 1)

    corner_pad = jnp.zeros((LANES - FACE, LANES), jnp.float32)
    for e in range(N):
        x, y, k = e // E // Y, e // E % Y, e % E
        piv_loads[e].wait()
        turned[0, e] = jnp.concatenate([piv[x, y, k, TAIL:, :LANES], corner_pad], 0).T[:FACE]
        turned[1, e] = jnp.concatenate([piv[x, y, k, :FACE, :LANES], corner_pad], 0).T[:FACE]
        turned[2, e] = jnp.concatenate([piv[x, y, k, :FACE, TAIL - 32 :], corner_pad], 0).T[32:]
    for c in loads[1:]:
        c.wait()
    if n_a + SY > 2:
        pl.semaphore_wait(barrier, n_a + SY - 2)

    def put(columns, e, column):
        return jnp.where(lane == e, column, columns)

    def rows_of(columns):
        return columns.T[:N]

    def remote(src, dst, send, recv, device):
        return pltpu.make_async_remote_copy(
            src_ref=src, dst_ref=dst, send_sem=send, recv_sem=recv, device_id=device, device_id_type=MESH
        )

    def halo_copies(j):
        s = halo_sem
        return [
            (sx < SX - 1, sx > 0, remote(dbuf.at[j, X - 1], hx_low.at[j], s.at[0, 0, j], s.at[1, 0, j], {"sx": lax.rem(sx + 1, SX)})),
            (sx > 0, sx < SX - 1, remote(dbuf.at[j, 0], hx_high.at[j], s.at[0, 1, j], s.at[1, 1, j], {"sx": lax.rem(sx + SX - 1, SX)})),
            (sy < SY - 1, sy > 0, remote(dbuf.at[j, :, Y - 1], hy_low.at[j], s.at[0, 2, j], s.at[1, 2, j], {"sy": lax.rem(sy + 1, SY)})),
            (sy > 0, sy < SY - 1, remote(dbuf.at[j, :, 0], hy_high.at[j], s.at[0, 3, j], s.at[1, 3, j], {"sy": lax.rem(sy + SY - 1, SY)})),
        ]

    def wall_copies(j):
        s = wall_sem
        return (
            remote(fwd_out.at[j], fwd_in.at[j], s.at[0, 0, j], s.at[1, 0, j], {"wall": lax.rem(wall + 1, W)}),
            remote(bwd_out.at[j], bwd_in.at[j], s.at[0, 1, j], s.at[1, 1, j], {"wall": lax.rem(wall + W - 1, W)}),
        )

    def step(j, carry):
        columns = jnp.zeros((BLOCK, LANES), jnp.float32)
        for e in range(N):
            x, y, k = e // E // Y, e // E % Y, e % E
            r = ubuf[j, e : e + 1, :]
            part = piv[x, y, k, :, :LANES] * r[:, :LANES]
            for c in range(1, BLOCK // LANES):
                part += piv[x, y, k, :, c * LANES : (c + 1) * LANES] * r[:, c * LANES : (c + 1) * LANES]
            columns = put(columns, e, jnp.sum(part, 1, keepdims=True))
        y_all = rows_of(columns)
        yrow[...] = y_all
        ahead = y_all[:, TAIL:]

        forward, backward = wall_copies(j)

        @pl.when(wall > 0)
        def _():
            forward.wait_recv()

        u_cols = [None] * N
        for l, (x, y) in enumerate(lines):
            s = fwd_in[j, l : l + 1, :FACE]
            for k in range(E):
                e = l * E + k
                u_cols[e] = jnp.sum(low[x, y, k] * s, 1, keepdims=True)
                s = ahead[e : e + 1] - jnp.sum(turned[0, e, :, :FACE] * u_cols[e], 0, keepdims=True)
            fwd_out[j, l : l + 1, :FACE] = s

        @pl.when(wall < W - 1)
        def _():
            forward.start()

        trailing = []
        u_columns = jnp.zeros((FACE, LANES), jnp.float32)
        for e in range(N):
            trailing.append(
                yrow[e : e + 1, :FACE] - jnp.sum(turned[1, e, :, :FACE] * u_cols[e], 0, keepdims=True)
            )
            u_columns = put(u_columns, e, u_cols[e])
        u_rows = rows_of(jnp.concatenate([u_columns, corner_pad], 0))

        @pl.when(wall < W - 1)
        def _():
            backward.wait_recv()

        v_columns = jnp.zeros((FACE, LANES), jnp.float32)
        for l, (x, y) in enumerate(lines):
            t = bwd_in[j, l : l + 1, :FACE]
            for k in reversed(range(E)):
                e = l * E + k
                v = jnp.sum(up[x, y, k] * t, 1, keepdims=True)
                v_columns = put(v_columns, e, v)
                t = trailing[e] - jnp.sum(turned[2, e, :, :FACE] * v, 0, keepdims=True)
            bwd_out[j, l : l + 1, :FACE] = t

        @pl.when(wall > 0)
        def _():
            backward.start()

        v_rows = rows_of(jnp.concatenate([corner_pad, v_columns], 0))
        columns = jnp.zeros((BLOCK, LANES), jnp.float32)
        for e in range(N):
            x, y, k = e // E // Y, e // E % Y, e % E
            part = piv[x, y, k, :, :LANES] * u_rows[e : e + 1]
            part += piv[x, y, k, :, BLOCK - LANES :] * v_rows[e : e + 1]
            columns = put(columns, e, jnp.sum(part, 1, keepdims=True))
        d = yrow[...] - rows_of(columns)
        for l, (x, y) in enumerate(lines):
            dbuf[j, x, y] = d[l * E : (l + 1) * E]

        halos = halo_copies(j)
        for sends, _, copy in halos:
            pl.when(sends)(copy.start)
        for _, receives, copy in halos:
            pl.when(receives)(copy.wait_recv)

        beside = [[], [], [], []]
        for x, y in lines:
            beside[0].append(dbuf[j, x - 1, y] if x > 0 else hx_low[j, y])
            beside[1].append(dbuf[j, x + 1, y] if x < X - 1 else hx_high[j, y])
            beside[2].append(dbuf[j, x, y - 1] if y > 0 else hy_low[j, x])
            beside[3].append(dbuf[j, x, y + 1] if y < Y - 1 else hy_high[j, x])
        turns = jnp.concatenate([ori[x, y] for x, y in lines], 0)
        blocks = []
        for f in range(4):
            all_turns = select_dot(jnp.concatenate(beside[f], 0), gat[f])
            across = all_turns[:, :LANES]
            for q in range(1, 4):
                across = jnp.where(turns[:, f : f + 1] == q, all_turns[:, q * LANES : (q + 1) * LANES], across)
            across = across[:, :FACE]
            block = jnp.zeros((FACE, LANES), jnp.float32)
            for e in range(N):
                x, y, k = e // E // Y, e // E % Y, e % E
                block = put(block, e, jnp.sum(side[x, y, k, f] * across[e : e + 1], 1, keepdims=True))
            blocks.append(block)
        coupled = rows_of(jnp.concatenate(blocks, 0))
        ubuf[j + 1] = select_dot(coupled, sca[...])
        return carry

    lax.fori_loop(0, ITERS, step, 0)

    sums = []
    for a, b in PAIRS:
        product = ubuf[a] * ubuf[b]
        folded = product[:, :LANES]
        for c in range(1, BLOCK // LANES):
            folded += product[:, c * LANES : (c + 1) * LANES]
        sums.append(jnp.sum(folded, 0, keepdims=True))
    sums.append(jnp.zeros((16 - len(PAIRS), LANES), jnp.float32))
    gram_a[rank] = jnp.concatenate(sums, 0)
    a_copies = [
        remote(gram_a.at[rank], gram_a.at[rank], a_send.at[t - 1], a_recv.at[t - 1], group_a(t)) for t in range(1, n_a)
    ]
    for c in a_copies:
        c.start()
    for t in range(1, n_a):
        source = lax.rem(rank + n_a - t, n_a)
        remote(gram_a.at[source], gram_a.at[source], a_send.at[t - 1], a_recv.at[t - 1], group_a(t)).wait_recv()
    gram = gram_a[0]
    for i in range(1, n_a):
        gram += gram_a[i]
    gram_b[sy] = gram
    b_copies = [
        remote(gram_b.at[sy], gram_b.at[sy], b_send.at[t - 1], b_recv.at[t - 1], group_b(t)) for t in range(1, SY)
    ]
    for c in b_copies:
        c.start()
    for t in range(1, SY):
        source = lax.rem(sy + SY - t, SY)
        remote(gram_b.at[source], gram_b.at[source], b_send.at[t - 1], b_recv.at[t - 1], group_b(t)).wait_recv()
    gram = gram_b[0]
    for i in range(1, SY):
        gram += gram_b[i]
    gram = jnp.sum(gram, 1, keepdims=True)
    g = {}
    for i, (a, b) in enumerate(PAIRS):
        g[a, b] = gram[i : i + 1]

    M = ITERS
    zero = jnp.zeros((1, 1), jnp.float32)
    tri = [[zero] * (M + 1) for _ in range(M + 1)]
    for i in range(M + 1):
        rest = g[i, i]
        for p in range(i):
            rest = rest - tri[p][i] * tri[p][i]
        tri[i][i] = jnp.sqrt(jnp.maximum(rest, 0.0))
        for c in range(i + 1, M + 1):
            rest = g[i, c]
            for p in range(i):
                rest = rest - tri[p][i] * tri[p][c]
            tri[i][c] = rest / tri[i][i]
    hess = [[zero] * M for _ in range(M + 1)]
    for i in range(M + 1):
        for c in range(M):
            value = tri[i][c + 1]
            for p in range(c):
                value = value - hess[i][p] * tri[p][c]
            hess[i][c] = value / tri[c][c]
    for c in range(M):
        hess[c][c] = hess[c][c] + 1.0
    for c in range(M):
        for i in range(c + 2, M + 1):
            hess[i][c] = zero
    start = tri[0][0]
    normal = [[zero] * M for _ in range(M)]
    for a in range(M):
        for b in range(a, M):
            value = hess[0][a] * hess[0][b]
            for i in range(1, M + 1):
                value = value + hess[i][a] * hess[i][b]
            normal[a][b] = normal[b][a] = value
    right = [hess[0][a] * start for a in range(M)]
    for k in range(M):
        for i in range(k + 1, M):
            factor = normal[i][k] / normal[k][k]
            for c in range(k, M):
                normal[i][c] = normal[i][c] - factor * normal[k][c]
            right[i] = right[i] - factor * right[k]
    weights = [zero] * M
    for k in reversed(range(M)):
        value = right[k]
        for c in range(k + 1, M):
            value = value - normal[k][c] * weights[c]
        weights[k] = value / normal[k][k]
    squared = zero
    for i in range(M + 1):
        miss = start if i == 0 else zero
        for c in range(M):
            miss = miss - hess[i][c] * weights[c]
        squared = squared + miss * miss
    rel_ref[0] = (jnp.sqrt(squared) / start)[0, 0]
    rms_ref[0] = jnp.sqrt(g[0, 0] / total_entries)[0, 0]
    mixed = [zero] * M
    for k in reversed(range(M)):
        value = weights[k]
        for c in range(k + 1, M):
            value = value - tri[k][c] * mixed[c]
        mixed[k] = value / tri[k][k]
    for x, y in lines:
        out = mixed[0] * dbuf[0, x, y]
        for k in range(1, M):
            out = out + mixed[k] * dbuf[k, x, y]
        sol_ref[x, y] = out

    for c in a_copies + b_copies:
        c.wait_send()
    for j in range(ITERS):
        forward, backward = wall_copies(j)
        pl.when(wall < W - 1)(forward.wait_send)
        pl.when(wall > 0)(backward.wait_send)
        for sends, _, copy in halo_copies(j):
            pl.when(sends)(copy.wait_send)


def shards(dims, forcing, pivot_inverse, lower_face, upper_face, side_coupling, orientation):
    W, SX, SY = dims
    X, Y, E = forcing.shape[:3]
    L, N = X * Y, X * Y * E
    total_entries = forcing.size * W * SX * SY
    gather = jnp.asarray(gather_matrices(), jnp.bfloat16)
    scatter = jnp.asarray(scatter_matrix(), jnp.bfloat16)
    operands = (forcing, pivot_inverse, lower_face, upper_face, side_coupling, orientation, gather, scatter)
    f32 = jnp.float32
    dma = pltpu.SemaphoreType.DMA
    solution_out, relative, rms = pl.pallas_call(
        functools.partial(kernel, dims, total_entries),
        out_shape=(
            jax.ShapeDtypeStruct(forcing.shape, f32),
            jax.ShapeDtypeStruct((1,), f32),
            jax.ShapeDtypeStruct((1,), f32),
        ),
        in_specs=[pl.BlockSpec(memory_space=pl.ANY)] * len(operands),
        out_specs=(
            pl.BlockSpec(memory_space=pltpu.VMEM),
            pl.BlockSpec(memory_space=pltpu.SMEM),
            pl.BlockSpec(memory_space=pltpu.SMEM),
        ),
        scratch_shapes=[pltpu.VMEM(a.shape, a.dtype) for a in operands]
        + [
            pltpu.VMEM((3, N, FACE, LANES), f32),
            pltpu.VMEM((ITERS + 1, N, BLOCK), f32),
            pltpu.VMEM((ITERS, X, Y, E, BLOCK), f32),
            pltpu.VMEM((N, BLOCK), f32),
            pltpu.VMEM((ITERS, L, LANES), f32),
            pltpu.VMEM((ITERS, L, LANES), f32),
            pltpu.VMEM((ITERS, L, LANES), f32),
            pltpu.VMEM((ITERS, L, LANES), f32),
            pltpu.VMEM((ITERS, Y, E, BLOCK), f32),
            pltpu.VMEM((ITERS, Y, E, BLOCK), f32),
            pltpu.VMEM((ITERS, X, E, BLOCK), f32),
            pltpu.VMEM((ITERS, X, E, BLOCK), f32),
            pltpu.VMEM((W * SX, 16, LANES), f32),
            pltpu.VMEM((SY, 16, LANES), f32),
            dma((7,)),
            dma((N,)),
            dma((2, 2, ITERS)),
            dma((2, 4, ITERS)),
            dma((max(W * SX - 1, 1),)),
            dma((max(W * SX - 1, 1),)),
            dma((max(SY - 1, 1),)),
            dma((max(SY - 1, 1),)),
        ],
        compiler_params=pltpu.CompilerParams(
            collective_id=0, has_side_effects=True, vmem_limit_bytes=40 * 1024 * 1024
        ),
    )(*operands)
    return solution_out, relative.reshape(()), rms.reshape(())


def solution(mesh):
    dims = (mesh.shape["wall"], mesh.shape["sx"], mesh.shape["sy"])
    return jax.shard_map(
        functools.partial(shards, dims),
        mesh=mesh,
        in_specs=(
            P("sx", "sy", "wall", None),
            P("sx", "sy", "wall", None, None),
            P("sx", "sy", "wall", None, None),
            P("sx", "sy", "wall", None, None),
            P("sx", "sy", "wall", None, None, None),
            P("sx", "sy", "wall", None),
        ),
        out_specs=(P("sx", "sy", "wall", None), P(), P()),
        check_vma=False,
    )
```

time: 711 us -> 59.6 us (0.08); the launches traced: 701 us -> 59.2 us
  blocking collectives: 425 us -> 0 us
  matrix products: 72.3 us -> 0 us
  other arithmetic: 71.4 us -> 0 us
  local copies, waits for them, and re-layouts: 62.6 us -> 10.1 us
  Pallas kernels: 0 us -> 44.8 us
  starting transfers between devices: 30.4 us -> 0 us
  waiting for transfers between devices: 24.3 us -> 0 us
  between operations: 14.3 us -> 4.22 us
    psum x10 -> x0, blocking collectives: 405 us -> none  [the longest x6 241 us: shards(): projected = lax.psum(jnp.sum(vector_w * krylov[i]), ('wall', 'sx', 'sy'))]
    dot_general x90 -> x0, matrix products: 72.3 us -> none  [the longest x65 21.5 us: apply_map(): return jnp.einsum('xyab,xyb->xya', matrix, vector, precision=precise)]
    pallas_call x0 -> x1, Pallas kernels: none -> 44.8 us  [shards(): pl.pallas_call(functools.partial(kernel, dims, total_entries), out_shape=...]
    ppermute x12 -> x0, starting transfers between devices: 30.4 us -> none  [the longest x6 22.4 us: extended(): lax.ppermute(lax.slice_in_dim(block, block.shape[dim] - width, None, axis...]
    ppermute x12 -> x0, waiting for transfers between devices: 24.3 us -> none  [the longest x6 24 us: extended(): lax.ppermute(lax.slice_in_dim(block, 0, width, axis=dim), axis, backward)]
    reduce_sum x13 -> x0, other arithmetic: 20.8 us -> none  [the longest x6 9.68 us: shards(): projected = lax.psum(jnp.sum(vector_w * krylov[i]), ('wall', 'sx', 'sy'))]
    all_gather x8 -> x0, blocking collectives: 19.4 us -> none  [entering(): gathered = jax.tree.map(lambda a: lax.all_gather(a, axis), part)]
    add x43 -> x0, other arithmetic: 15.5 us -> none  [the longest x18 5.52 us: shards(): ahead_part[:, :, precondition_i]]
  transfers between devices with their start and end apart: 12 -> 0, of which waited for: 9 -> 0; matrix products, arithmetic and copies ran while one was open for 0% -> 0% of each run, Pallas kernels for 0% -> 0%
where the time goes in v1:
time: 59.6 us; the launch traced here: 59.2 us
  Pallas kernels  44.8 us (75%)
  local copies, waits for them, and re-layouts  10.1 us (17%)
  between operations  4.22 us (7%)
    pallas_call x1, Pallas kernels, shards(): pl.pallas_call(functools.partial(kernel, dims, total_entries), out_shape=...  44.8 us
    unnamed x17, local copies, waits for them, and re-layouts  10.1 us

profile of v1, /device:TPU:0, one launch (start us, length us, event | category | flops | bytes accessed | tf_op | source)
XLA Modules:
  0.0 59.2 jit_solution(9145625135972190840)
XLA Ops:
  0.6 0.0 copy-start
  0.6 2.3 %copy-done = f32[1,2,4,384,384]{4,3,2,1,0:T(8,128)S(1)} copy-done((f32[1,2,4,384,384]{4,3,2,1,0:T(8,128)S(1)}, f32[1,2,4,384,384]{4,3,2,1,0:T(8,128)}, u32[]{:S(2)}) %copy-start) | copy-done | bytes 4718616
  3.0 0.0 copy-start.1
  3.0 1.4 %copy-done.1 = f32[1,2,4,4,96,96]{5,4,3,2,1,0:T(8,128)S(1)} copy-done((f32[1,2,4,4,96,96]{5,4,3,2,1,0:T(8,128)S(1)}, f32[1,2,4,4,96,96]{5,4,3,2,1,0:T(8,128)}, u32[]{:S(2)}) %copy-start.1) | copy-done | bytes 1179672
  4.4 0.0 copy-start.2
  4.4 1.4 %copy-done.2 = bf16[4,384,512]{2,1,0:T(8,128)(2,1)S(1)} copy-done((bf16[4,384,512]{2,1,0:T(8,128)(2,1)S(1)}, bf16[4,384,512]{2,1,0:T(8,128)(2,1)}, u32[]{:S(2)}) %copy-start.2) | copy-done | bytes 1572888
  5.8 0.0 copy-start.3
  5.8 1.0 %copy-done.3 = f32[1,2,4,96,96]{4,3,2,1,0:T(8,128)S(1)} copy-done((f32[1,2,4,96,96]{4,3,2,1,0:T(8,128)S(1)}, f32[1,2,4,96,96]{4,3,2,1,0:T(8,128)}, u32[]{:S(2)}) %copy-start.3) | copy-done | bytes 294936
  6.8 0.0 copy-start.4
  6.8 1.0 %copy-done.4 = f32[1,2,4,96,96]{4,3,2,1,0:T(8,128)S(1)} copy-done((f32[1,2,4,96,96]{4,3,2,1,0:T(8,128)S(1)}, f32[1,2,4,96,96]{4,3,2,1,0:T(8,128)}, u32[]{:S(2)}) %copy-start.4) | copy-done | bytes 294936
  7.8 0.0 copy-start.5
  7.8 1.0 %copy-done.5 = bf16[384,384]{1,0:T(8,128)(2,1)S(1)} copy-done((bf16[384,384]{1,0:T(8,128)(2,1)S(1)}, bf16[384,384]{1,0:T(8,128)(2,1)}, u32[]{:S(2)}) %copy-start.5) | copy-done | bytes 294936
  8.7 0.0 copy-start.6
  8.7 0.7 %copy-done.6 = f32[1,2,4,384]{3,2,1,0:T(4,128)S(1)} copy-done((f32[1,2,4,384]{3,2,1,0:T(4,128)S(1)}, f32[1,2,4,384]{3,2,1,0:T(4,128)}, u32[]{:S(2)}) %copy-start.6) | copy-done | bytes 12312
  9.4 0.0 copy-start.7
  9.4 0.7 %copy-done.7 = s32[1,2,4,4]{3,2,1,0:T(4,128)S(1)} copy-done((s32[1,2,4,4]{3,2,1,0:T(4,128)S(1)}, s32[1,2,4,4]{3,2,1,0:T(4,128)}, u32[]{:S(2)}) %copy-start.7) | copy-done | bytes 152
  10.1 44.8 %shard_map.103 = (f32[1,2,4,384]{3,2,1,0:T(4,128)S(1)}, f32[1]{0:T(128)}, f32[1]{0:T(128)}) custom-call(f32[1,2,4,384]{3,2,1,0:T(4,128)S(1)} %copy-done.6, f32[1,2,4,384,384]{4,3,2,1,0:T(8,128)S(1)} %copy-done, f32[1,2,4,96,96]{4,3,2,1,0:T(8,128)S(1)} %copy-done.3, f32[1,2,4,96,96]{4,3,2,1,0:T(8,128)S(1)} %copy-done.4, ...), custom_call_target="tpu_custom_call" | custom-call | tf_op jit(solution)/shard_map/pallas_call | solution.py:422
  55.0 0.6 %copy.14 = f32[1,2,4,384]{3,2,1,0:T(4,128)} copy(f32[1,2,4,384]{3,2,1,0:T(4,128)S(1)} %get-tuple-element.12) | data formatting | bytes 24576
Async XLA Ops:
  0.6 2.3 %copy-start = (f32[1,2,4,384,384]{4,3,2,1,0:T(8,128)S(1)}, f32[1,2,4,384,384]{4,3,2,1,0:T(8,128)}, u32[]{:S(2)}) copy-start(f32[1,2,4,384,384]{4,3,2,1,0:T(8,128)} %piv_hbm.1) | copy-start | bytes 14155780
  3.0 1.4 %copy-start.1 = (f32[1,2,4,4,96,96]{5,4,3,2,1,0:T(8,128)S(1)}, f32[1,2,4,4,96,96]{5,4,3,2,1,0:T(8,128)}, u32[]{:S(2)}) copy-start(f32[1,2,4,4,96,96]{5,4,3,2,1,0:T(8,128)} %side_hbm.1) | copy-start | bytes 3538948
  4.4 1.4 %copy-start.2 = (bf16[4,384,512]{2,1,0:T(8,128)(2,1)S(1)}, bf16[4,384,512]{2,1,0:T(8,128)(2,1)}, u32[]{:S(2)}) copy-start(bf16[4,384,512]{2,1,0:T(8,128)(2,1)} %constant.4.clone.gat_hbm) | copy-start | bytes 4718596
  5.8 1.0 %copy-start.3 = (f32[1,2,4,96,96]{4,3,2,1,0:T(8,128)S(1)}, f32[1,2,4,96,96]{4,3,2,1,0:T(8,128)}, u32[]{:S(2)}) copy-start(f32[1,2,4,96,96]{4,3,2,1,0:T(8,128)} %low_hbm.1) | copy-start | bytes 884740
  6.8 1.0 %copy-start.4 = (f32[1,2,4,96,96]{4,3,2,1,0:T(8,128)S(1)}, f32[1,2,4,96,96]{4,3,2,1,0:T(8,128)}, u32[]{:S(2)}) copy-start(f32[1,2,4,96,96]{4,3,2,1,0:T(8,128)} %up_hbm.1) | copy-start | bytes 884740
  7.8 1.0 %copy-start.5 = (bf16[384,384]{1,0:T(8,128)(2,1)S(1)}, bf16[384,384]{1,0:T(8,128)(2,1)}, u32[]{:S(2)}) copy-start(bf16[384,384]{1,0:T(8,128)(2,1)} %constant.5.clone.sca_hbm) | copy-start | bytes 884740
  8.7 0.7 %copy-start.6 = (f32[1,2,4,384]{3,2,1,0:T(4,128)S(1)}, f32[1,2,4,384]{3,2,1,0:T(4,128)}, u32[]{:S(2)}) copy-start(f32[1,2,4,384]{3,2,1,0:T(4,128)} %f_hbm.1) | copy-start | bytes 36868
  9.4 0.7 %copy-start.7 = (s32[1,2,4,4]{3,2,1,0:T(4,128)S(1)}, s32[1,2,4,4]{3,2,1,0:T(4,128)}, u32[]{:S(2)}) copy-start(s32[1,2,4,4]{3,2,1,0:T(4,128)} %ori_hbm.1) | copy-start | bytes 388

commit v2 on v1

--- a/solution.py
+++ b/solution.py
@@ -54,6 +54,21 @@
     rows = x.shape[0]
     y = jnp.dot(split_rows(x), chosen, preferred_element_type=jnp.float32)
     return y[:rows] + y[rows : 2 * rows] + y[2 * rows : 3 * rows]
+
+
+def lane_sums(part):
+    high = part.astype(jnp.bfloat16)
+    low = (part - high.astype(jnp.float32)).astype(jnp.bfloat16)
+    ones = jnp.ones((16, part.shape[1]), jnp.bfloat16)
+    if part.shape[1] == LANES:
+        high, low = jnp.concatenate([high, low], 1), None
+        ones = jnp.ones((16, 2 * LANES), jnp.bfloat16)
+
+    def total(rows):
+        return lax.dot_general(ones, rows, (((1,), (1,)), ((), ())), preferred_element_type=jnp.float32)
+
+    sums = total(high)
+    return (sums if low is None else sums + total(low))[:1]
 
 
 def kernel(
@@ -171,6 +186,11 @@
     def put(columns, e, column):
         return jnp.where(lane == e, column, columns)
 
+    row_ids = lax.broadcasted_iota(jnp.int32, (N, 1), 0)
+
+    def put_row(rows, e, row):
+        return jnp.where(row_ids == e, row, rows)
+
     def rows_of(columns):
         return columns.T[:N]
 
@@ -196,15 +216,14 @@
         )
 
     def step(j, carry):
-        columns = jnp.zeros((BLOCK, LANES), jnp.float32)
+        y_all = jnp.zeros((N, BLOCK), jnp.float32)
         for e in range(N):
             x, y, k = e // E // Y, e // E % Y, e % E
             r = ubuf[j, e : e + 1, :]
             part = piv[x, y, k, :, :LANES] * r[:, :LANES]
             for c in range(1, BLOCK // LANES):
                 part += piv[x, y, k, :, c * LANES : (c + 1) * LANES] * r[:, c * LANES : (c + 1) * LANES]
-            columns = put(columns, e, jnp.sum(part, 1, keepdims=True))
-        y_all = rows_of(columns)
+            y_all = put_row(y_all, e, lane_sums(part))
         yrow[...] = y_all
         ahead = y_all[:, TAIL:]
 
@@ -255,13 +274,13 @@
             backward.start()
 
         v_rows = rows_of(jnp.concatenate([corner_pad, v_columns], 0))
-        columns = jnp.zeros((BLOCK, LANES), jnp.float32)
+        change = jnp.zeros((N, BLOCK), jnp.float32)
         for e in range(N):
             x, y, k = e // E // Y, e // E % Y, e % E
             part = piv[x, y, k, :, :LANES] * u_rows[e : e + 1]
             part += piv[x, y, k, :, BLOCK - LANES :] * v_rows[e : e + 1]
-            columns = put(columns, e, jnp.sum(part, 1, keepdims=True))
-        d = yrow[...] - rows_of(columns)
+            change = put_row(change, e, lane_sums(part))
+        d = yrow[...] - change
         for l, (x, y) in enumerate(lines):
             dbuf[j, x, y] = d[l * E : (l + 1) * E]
 
@@ -278,19 +297,18 @@
             beside[2].append(dbuf[j, x, y - 1] if y > 0 else hy_low[j, x])
             beside[3].append(dbuf[j, x, y + 1] if y < Y - 1 else hy_high[j, x])
         turns = jnp.concatenate([ori[x, y] for x, y in lines], 0)
-        blocks = []
+        picked = []
         for f in range(4):
             all_turns = select_dot(jnp.concatenate(beside[f], 0), gat[f])
             across = all_turns[:, :LANES]
             for q in range(1, 4):
                 across = jnp.where(turns[:, f : f + 1] == q, all_turns[:, q * LANES : (q + 1) * LANES], across)
-            across = across[:, :FACE]
-            block = jnp.zeros((FACE, LANES), jnp.float32)
-            for e in range(N):
-                x, y, k = e // E // Y, e // E % Y, e % E
-                block = put(block, e, jnp.sum(side[x, y, k, f] * across[e : e + 1], 1, keepdims=True))
-            blocks.append(block)
-        coupled = rows_of(jnp.concatenate(blocks, 0))
+            picked.append(across[:, :FACE])
+        coupled = jnp.zeros((N, 4 * FACE), jnp.float32)
+        for e in range(N):
+            x, y, k = e // E // Y, e // E % Y, e % E
+            part = jnp.concatenate([side[x, y, k, f] * picked[f][e : e + 1] for f in range(4)], 0)
+            coupled = put_row(coupled, e, lane_sums(part))
         ubuf[j + 1] = select_dot(coupled, sca[...])
         return carry
 
@@ -426,7 +444,7 @@
             jax.ShapeDtypeStruct((1,), f32),
             jax.ShapeDtypeStruct((1,), f32),
         ),
-        in_specs=[pl.BlockSpec(memory_space=pl.ANY)] * len(operands),
+        in_specs=[pl.BlockSpec(memory_space=pltpu.HBM)] * len(operands),
         out_specs=(
             pl.BlockSpec(memory_space=pltpu.VMEM),
             pl.BlockSpec(memory_space=pltpu.SMEM),
@@ -458,7 +476,7 @@
             dma((max(SY - 1, 1),)),
         ],
         compiler_params=pltpu.CompilerParams(
-            collective_id=0, has_side_effects=True, vmem_limit_bytes=40 * 1024 * 1024
+            collective_id=0, has_side_effects=True, vmem_limit_bytes=60 * 1024 * 1024
         ),
     )(*operands)
     return solution_out, relative.reshape(()), rms.reshape(())

time: 59.6 us -> 51.4 us (0.86)
  local copies, waits for them, and re-layouts: 10.1 us -> 1.31 us
  Pallas kernels: 44.8 us -> 45.6 us
    unnamed x17 -> x1, local copies, waits for them, and re-layouts: 10.1 us -> 1.31 us
    pallas_call x1, Pallas kernels: 44.8 us -> 45.6 us  [shards(): pl.pallas_call(functools.partial(kernel, dims, total_entries), out_shape=...]
where the time goes in v2:
time: 51.4 us; the launch traced here: 51.1 us
  Pallas kernels  45.6 us (89%)
  between operations  4.16 us (8%)
  local copies, waits for them, and re-layouts  1.31 us (3%)
    pallas_call x1, Pallas kernels, shards(): pl.pallas_call(functools.partial(kernel, dims, total_entries), out_shape=...  45.6 us
    unnamed x1, local copies, waits for them, and re-layouts  1.31 us

profile of v2, /device:TPU:0, one launch (start us, length us, event | category | flops | bytes accessed | tf_op | source)
XLA Modules:
  0.0 51.1 jit_solution(17857714507115288781)
XLA Ops:
  0.6 45.6 %shard_map.103 = (f32[1,2,4,384]{3,2,1,0:T(4,128)}, f32[1]{0:T(128)}, f32[1]{0:T(128)}) custom-call(f32[1,2,4,384]{3,2,1,0:T(4,128)} %f_hbm.1, f32[1,2,4,384,384]{4,3,2,1,0:T(8,128)} %piv_hbm.1, f32[1,2,4,96,96]{4,3,2,1,0:T(8,128)} %low_hbm.1, f32[1,2,4,96,96]{4,3,2,1,0:T(8,128)} %up_hbm.1, f32[1,2,4,4,96,96]{5,4,3,2,1,0:T(8,128)} %side_hbm.1, ...), custom_call_target="tpu_custom_call" | custom-call | tf_op jit(solution)/shard_map/pallas_call | solution.py:440
  46.3 1.3 %copy.14 = f32[1,2,4,384]{3,2,1,0:T(4,128)} copy(f32[1,2,4,384]{3,2,1,0:T(4,128)} %get-tuple-element.12) | data formatting | bytes 24576

commit v3 on v2

--- a/solution.py
+++ b/solution.py
@@ -234,13 +234,15 @@
             forward.wait_recv()
 
         u_cols = [None] * N
-        for l, (x, y) in enumerate(lines):
-            s = fwd_in[j, l : l + 1, :FACE]
-            for k in range(E):
+        s = [fwd_in[j, l : l + 1, :FACE] for l in range(L)]
+        for k in range(E):
+            for l, (x, y) in enumerate(lines):
+                u_cols[l * E + k] = jnp.sum(low[x, y, k] * s[l], 1, keepdims=True)
+            for l in range(L):
                 e = l * E + k
-                u_cols[e] = jnp.sum(low[x, y, k] * s, 1, keepdims=True)
-                s = ahead[e : e + 1] - jnp.sum(turned[0, e, :, :FACE] * u_cols[e], 0, keepdims=True)
-            fwd_out[j, l : l + 1, :FACE] = s
+                s[l] = ahead[e : e + 1] - jnp.sum(turned[0, e, :, :FACE] * u_cols[e], 0, keepdims=True)
+        for l in range(L):
+            fwd_out[j, l : l + 1, :FACE] = s[l]
 
         @pl.when(wall < W - 1)
         def _():
@@ -260,14 +262,15 @@
             backward.wait_recv()
 
         v_columns = jnp.zeros((FACE, LANES), jnp.float32)
-        for l, (x, y) in enumerate(lines):
-            t = bwd_in[j, l : l + 1, :FACE]
-            for k in reversed(range(E)):
+        t = [bwd_in[j, l : l + 1, :FACE] for l in range(L)]
+        for k in reversed(range(E)):
+            v = [jnp.sum(up[x, y, k] * t[l], 1, keepdims=True) for l, (x, y) in enumerate(lines)]
+            for l in range(L):
                 e = l * E + k
-                v = jnp.sum(up[x, y, k] * t, 1, keepdims=True)
-                v_columns = put(v_columns, e, v)
-                t = trailing[e] - jnp.sum(turned[2, e, :, :FACE] * v, 0, keepdims=True)
-            bwd_out[j, l : l + 1, :FACE] = t
+                v_columns = put(v_columns, e, v[l])
+                t[l] = trailing[e] - jnp.sum(turned[2, e, :, :FACE] * v[l], 0, keepdims=True)
+        for l in range(L):
+            bwd_out[j, l : l + 1, :FACE] = t[l]
 
         @pl.when(wall > 0)
         def _():

time: 51.4 us -> 51.4 us (level)
  no operation moved by 1% of the time
where the time goes in v3:
time: 51.4 us; the launch traced here: 51.1 us
  Pallas kernels  45.7 us (89%)
  between operations  4.16 us (8%)
  local copies, waits for them, and re-layouts  1.31 us (3%)
    pallas_call x1, Pallas kernels, shards(): pl.pallas_call(functools.partial(kernel, dims, total_entries), out_shape=...  45.7 us
    unnamed x1, local copies, waits for them, and re-layouts  1.31 us

profile of v3, /device:TPU:0, one launch (start us, length us, event | category | flops | bytes accessed | tf_op | source)
XLA Modules:
  0.0 51.1 jit_solution(6996352709752579202)
XLA Ops:
  0.6 45.7 %shard_map.103 = (f32[1,2,4,384]{3,2,1,0:T(4,128)}, f32[1]{0:T(128)}, f32[1]{0:T(128)}) custom-call(f32[1,2,4,384]{3,2,1,0:T(4,128)} %f_hbm.1, f32[1,2,4,384,384]{4,3,2,1,0:T(8,128)} %piv_hbm.1, f32[1,2,4,96,96]{4,3,2,1,0:T(8,128)} %low_hbm.1, f32[1,2,4,96,96]{4,3,2,1,0:T(8,128)} %up_hbm.1, f32[1,2,4,4,96,96]{5,4,3,2,1,0:T(8,128)} %side_hbm.1, ...), custom_call_target="tpu_custom_call" | custom-call | tf_op jit(solution)/shard_map/pallas_call | solution.py:443
  46.3 1.3 %copy.14 = f32[1,2,4,384]{3,2,1,0:T(4,128)} copy(f32[1,2,4,384]{3,2,1,0:T(4,128)} %get-tuple-element.12) | data formatting | bytes 24576
